TPU v7x, 256 devices: a whole 4x4x8 slice. The times are simulated.
256 devices in a mesh: ctx: 64 (over y, x_lo, z), tp: 4 (over x_hi, core).
Axes of the slice: x: 4 (x_hi: 2, x_lo: 2; x = x_hi * 2 + x_lo), y: 4, z: 8, core: 2. Of those that a mesh axis runs over, the one named last changes fastest.
Arguments:
- queries: bfloat16 [16384, 4096], P('ctx', 'tp'), may hold values from -8 to 8
- latent_keys: bfloat16 [512, 4096], P(('ctx', 'tp')), may hold values from -8 to 8
- latent_values: bfloat16 [512, 4096], P(('ctx', 'tp')), may hold values from -6 to 6
- gate_logit: float32 [], replicated, may hold values from 0.3 to 1.2
- last_frame: int32 [128], P('ctx'), may hold values from 0 to 7, as said below
- cotangent: bfloat16 [16384, 4096], P('ctx', 'tp'), may hold values from -6 to 6
Outputs:
- attended: bfloat16 [16384, 4096], P('ctx', 'tp')
- query_grad: bfloat16 [16384, 4096], P('ctx', 'tp')
- key_grad: float32 [512, 4096], P(('ctx', 'tp'))
- value_grad: float32 [512, 4096], P(('ctx', 'tp'))
Inputs may be any that keep to these rules, and one draw needn't show every extreme that they name: Non-decreasing along the document; text block b sees the frames 0 to last_frame[b].
All inputs are finite; a program needn't handle non-finite values.
Results may differ from a plain program's by a relative error of at most 0.015.
Values may be sent and summed in bfloat16 or wider, within the bound.
No kernel may reach another device: no remote copies, remote signals or barrier semaphores. Data moves between devices by JAX's collectives and lax.ppermute only.
A program may use at most 64 MiB of HBM per device.

v0:
```python
import jax
import jax.numpy as jnp
from jax import lax
from jax.sharding import PartitionSpec as P

DH = 128
LATF = 64
TBLK = 128
masked_fill = -1e30


def per_device(queries, latent_keys, latent_values, gate_logit, last_frame, cotangent):
    tok_rows, columns = queries.shape
    head_count = columns // DH
    keys_every, values_every = (
        lax.all_gather(latent_keys, ("ctx", "tp"), axis=0, tiled=True),
        lax.all_gather(latent_values, ("ctx", "tp"), axis=0, tiled=True),
    )
    offset = lax.axis_index("tp") * columns
    keys_mine = lax.dynamic_slice_in_dim(keys_every, offset, columns, 1)
    values_mine = lax.dynamic_slice_in_dim(values_every, offset, columns, 1)
    latent_count = keys_mine.shape[0]
    keys_heads = keys_mine.reshape(latent_count, head_count, DH)
    values_heads = values_mine.reshape(latent_count, head_count, DH)
    score_scale = 1.0 / DH**0.5
    gate_value = jnp.tanh(gate_logit)
    frame_index = jnp.arange(latent_count, dtype=jnp.int32) // LATF
    last_tok = jnp.repeat(last_frame, TBLK, total_repeat_length=tok_rows)
    block_rows = min(512, tok_rows)
    block_count = tok_rows // block_rows

    def advance(running, block_index):
        row_start = block_index * block_rows
        query_block = queries.reshape(block_rows, head_count, DH)
        last_block = lax.dynamic_slice_in_dim(last_tok, row_start, block_rows, 0)
        visible = frame_index[None, :] <= last_block[:, None]
        scores = (
            jnp.einsum("qhd,khd->hqk", query_block, keys_heads, preferred_element_type=jnp.float32)
            * score_scale
        )
        scores = jnp.where(visible[None], scores, masked_fill)
        maxima = jnp.max(scores, axis=-1, keepdims=True)
        expo = jnp.where(visible[None], jnp.exp(scores - maxima), 0.0)
        totals = jnp.sum(expo, axis=-1, keepdims=True)
        weights = expo / totals
        weights_low = weights.astype(jnp.bfloat16)
        context = jnp.einsum(
            "hqk,khd->qhd", weights_low, values_heads, preferred_element_type=jnp.float32
        )
        attended = (gate_value * context.reshape(block_rows, columns)).astype(jnp.bfloat16)
        gated_cot = (gate_value * cotangent.astype(jnp.float32)).astype(jnp.bfloat16)
        gated_heads = gated_cot.reshape(block_rows, head_count, DH)
        prob_grad = jnp.einsum(
            "qhd,khd->hqk", gated_heads, values_heads, preferred_element_type=jnp.float32
        )
        inner_sum = jnp.sum(weights * prob_grad, axis=-1, keepdims=True)
        score_grad = (weights * (prob_grad - inner_sum) * score_scale).astype(jnp.bfloat16)
        query_grad = jnp.einsum(
            "hqk,khd->qhd", score_grad, keys_heads, preferred_element_type=jnp.float32
        )
        key_part = jnp.einsum(
            "hqk,qhd->khd", score_grad, query_block, preferred_element_type=jnp.float32
        )
        value_part = jnp.einsum(
            "hqk,qhd->khd", weights_low, gated_heads, preferred_element_type=jnp.float32
        )
        query_low = query_grad.reshape(block_rows, columns).astype(jnp.bfloat16)
        return ((running[0] + key_part, running[1] + value_part), (attended, query_low))

    zeros_kv = jnp.zeros((latent_count, head_count, DH), jnp.float32)
    sums, outputs = lax.scan(
        advance, (zeros_kv, zeros_kv), jnp.arange(block_count, dtype=jnp.int32)
    )
    attended = outputs[0].reshape(tok_rows, columns)
    query_grad = outputs[1].reshape(tok_rows, columns)
    key_terms = sums[0].reshape(latent_count, columns)
    value_terms = sums[1].reshape(latent_count, columns)
    key_total, value_total = lax.psum((key_terms, value_terms), "ctx")
    portion = latent_count // lax.axis_size("ctx")
    first_row = lax.axis_index("ctx") * portion
    key_own = lax.dynamic_slice_in_dim(key_total, first_row, portion, 0)
    value_own = lax.dynamic_slice_in_dim(value_total, first_row, portion, 0)
    key_grad, value_grad = (
        lax.all_to_all(
            key_own.astype(jnp.bfloat16), "tp", split_axis=0, concat_axis=1, tiled=True
        ).astype(key_own.dtype),
        lax.all_to_all(
            value_own.astype(jnp.bfloat16), "tp", split_axis=0, concat_axis=1, tiled=True
        ).astype(value_own.dtype),
    )
    return (attended, query_grad, key_grad, value_grad)


def solution(mesh):
    placed = (
        P("ctx", "tp"),
        P(("ctx", "tp"), None),
        P(("ctx", "tp"), None),
        P(),
        P("ctx"),
        P("ctx", "tp"),
    )
    return jax.shard_map(
        per_device,
        mesh=mesh,
        in_specs=placed,
        out_specs=(P("ctx", "tp"), P("ctx", "tp"), P(("ctx", "tp"), None), P(("ctx", "tp"), None)),
        check_vma=False,
    )
```

profile of v0, /device:TPU:1, one launch (start us, length us, event | category | flops | bytes accessed | tf_op | source)
XLA Modules:
  0.0 1265.6 jit_solution(15816836092543142598)
XLA Ops:
  7.2 0.7 all-gather.7.cloned.1.call-update
  7.9 0.7 all-gather.5.cloned.1.call-update
  9.3 2.0 copy.89
  11.4 1.1 multiply_convert_fusion.1
  12.5 1.0 copy.90
  13.5 1.3 fusion.37
  14.9 1.3 compare_select_fusion.1
  16.3 410.5 %all-gather.7.cloned.1.call-done = bf16[256,2,4096]{2,1,0:T(2,128)(2,1)} async-done(((bf16[1,2,4096]{2,1,0:T(2,128)(2,1)}), bf16[256,2,4096]{2,1,0:T(2,128)(2,1)}) %all-gather.7.cloned.1.call-update) | async-done | bytes 4194320 | tf_op jit(solution)/shard_map/all_gather | solution.py:16
  426.8 7.2 reshape.212
  434.0 406.2 %all-gather.5.cloned.1.call-done = bf16[256,2,4096]{2,1,0:T(2,128)(2,1)} async-done(((bf16[1,2,4096]{2,1,0:T(2,128)(2,1)}), bf16[256,2,4096]{2,1,0:T(2,128)(2,1)}) %all-gather.5.cloned.1.call-update) | async-done | bytes 4194320 | tf_op jit(solution)/shard_map/all_gather | solution.py:17
  840.2 7.2 reshape.210
  847.4 1.7 constant_dynamic-slice_fusion
  850.3 4.2 fusion.39
  854.5 3.8 fusion.38
  858.3 3.6 fusion.17
  861.9 2.2 fusion.21
  864.1 8.6 fusion.7
  872.7 1.9 copy.75
  874.6 3.0 copy.78
  877.6 302.5 %all-reduce.2 = (bf16[512,1024]{1,0:T(8,128)(2,1)}, bf16[512,1024]{1,0:T(8,128)(2,1)}) all-reduce(f32[512,1024]{1,0:T(8,128)S(1)} %copy.75, f32[512,1024]{1,0:T(8,128)} %copy.78), channel_id=1, replica_groups=mesh['ctx'=64,'tp'=4] {'ctx'}, use_global_device_ids=true, to_apply=%region_3.4 | all-reduce | flops 1048576 | bytes 6291456 | tf_op jit(solution)/shard_map/psum | solution.py:78
  1180.1 0.7 dynamic-slice_convert_fusion.1
  1180.8 0.6 all_to_all.20
  1181.4 58.1 %all-to-all-start = ((bf16[4,2,1024]{2,1,0:T(2,128)(2,1)}), bf16[4,2,1024]{2,1,0:T(2,128)(2,1)S(1)}, u32[]{:S(2)}, u32[]{:S(2)}) async-start(bf16[4,2,1024]{2,1,0:T(2,128)(2,1)} %all_to_all.20), calls=%async_computation | async-start | bytes 32768 | tf_op jit(solution)/shard_map/all_to_all | solution.py:84
  1239.5 0.7 dynamic-slice_convert_fusion
  1240.2 0.6 all_to_all.22
  1240.9 3.3 all-to-all-done
  1244.2 4.0 all-to-all-start.1
  1248.1 7.4 fusion.18
  1255.5 1.0 copy.79
  1256.5 1.0 copy.80
  1257.5 0.6 convert_element_type.82
  1258.1 0.6 convert_element_type.83
  (22 shorter events, 1.4 us)
Async XLA Ops:
  7.2 419.6 %all-gather.7.cloned.1.call-start = ((), (), s32[]{:S(2)}) async-start(), calls=%async_computation.3 | async-start | bytes 4210688 | tf_op jit(solution)/shard_map/all_gather | solution.py:16
  7.9 832.3 %all-gather.5.cloned.1.call-start = ((), (), s32[]{:S(2)}) async-start(), calls=%async_computation.2 | async-start | bytes 4210688 | tf_op jit(solution)/shard_map/all_gather | solution.py:17
  850.3 8.0 copy-start.1
  850.3 4.2 copy-start.3
  858.3 3.6 copy-start
  858.3 3.6 copy-start.5
  874.6 373.5 %copy-start.2 = (bf16[512,1024]{0,1:T(8,128)(2,1)S(1)}, bf16[512,1024]{0,1:T(8,128)(2,1)}, u32[]{:S(2)}) copy-start(bf16[512,1024]{0,1:T(8,128)(2,1)} %copy-done.1) | copy-start | bytes 3145732
  1181.4 62.8 %all-to-all-start = ((bf16[4,2,1024]{2,1,0:T(2,128)(2,1)}), bf16[4,2,1024]{2,1,0:T(2,128)(2,1)S(1)}, u32[]{:S(2)}, u32[]{:S(2)}) async-start(bf16[4,2,1024]{2,1,0:T(2,128)(2,1)} %all_to_all.20), calls=%async_computation | async-start | bytes 32768 | tf_op jit(solution)/shard_map/all_to_all | solution.py:84
  1244.2 14.0 %all-to-all-start.1 = ((bf16[4,2,1024]{2,1,0:T(2,128)(2,1)}), bf16[4,2,1024]{2,1,0:T(2,128)(2,1)S(1)}, u32[]{:S(2)}, u32[]{:S(2)}) async-start(bf16[4,2,1024]{2,1,0:T(2,128)(2,1)} %all_to_all.22), calls=%async_computation.1 | async-start | bytes 32768 | tf_op jit(solution)/shard_map/all_to_all | solution.py:87
  1248.1 7.4 copy-start.4
Sparse Core Ops, SparseCore 0:
  9.9 416.8 all-gather.6
  428.7 411.5 all-gather.4
where the time goes:
time: 1270 us
  waiting for transfers between devices  821 us (65%)
  blocking collectives  302 us (24%)
  starting transfers between devices  62.1 us (5%)
  local copies, waits for them, and re-layouts  31.2 us (2%)
  matrix products  29.7 us (2%)
  between operations  14.8 us (1%)
    all_gather x1, waiting for transfers between devices, per_device(): lax.all_gather(latent_keys, ('ctx', 'tp'), axis=0, tiled=True)  410 us
    all_gather x1, waiting for transfers between devices, per_device(): lax.all_gather(latent_values, ('ctx', 'tp'), axis=0, tiled=True)  406 us
    psum x1, blocking collectives, per_device(): key_total, value_total = lax.psum((key_terms, value_terms), 'ctx')  302 us
    all_to_all x1, starting transfers between devices, per_device(): lax.all_to_all(key_own.astype(jnp.bfloat16), 'tp', split_axis=0, concat_a...  58.1 us
  transfers between devices with their start and end apart: 4, of which 3 were waited for; matrix products, arithmetic and copies ran while one was open for 2% of the time, Pallas kernels for 0%

commit v1 on v0

--- a/solution.py
+++ b/solution.py
@@ -81,8 +81,14 @@
     key_own = lax.dynamic_slice_in_dim(key_total, first_row, portion, 0)
     value_own = lax.dynamic_slice_in_dim(value_total, first_row, portion, 0)
     key_grad, value_grad = (
-        lax.all_to_all(
-            key_own.astype(jnp.bfloat16), "tp", split_axis=0, concat_axis=1, tiled=True
+        jnp.concatenate(
+            lax.all_to_all(
+                jnp.stack(jnp.split(key_own.astype(jnp.bfloat16), lax.axis_size("tp"), axis=0)),
+                "tp",
+                0,
+                0,
+            ),
+            axis=1,
         ).astype(key_own.dtype),
         lax.all_to_all(
             value_own.astype(jnp.bfloat16), "tp", split_axis=0, concat_axis=1, tiled=True

time: 1270 us -> 1270 us (level)
  no operation moved by 1% of the time
where the time goes in v1:
time: 1270 us
  waiting for transfers between devices  821 us (65%)
  blocking collectives  302 us (24%)
  starting transfers between devices  62.1 us (5%)
  local copies, waits for them, and re-layouts  30.6 us (2%)
  matrix products  29.7 us (2%)
  between operations  14.8 us (1%)
    all_gather x1, waiting for transfers between devices, per_device(): lax.all_gather(latent_keys, ('ctx', 'tp'), axis=0, tiled=True)  410 us
    all_gather x1, waiting for transfers between devices, per_device(): lax.all_gather(latent_values, ('ctx', 'tp'), axis=0, tiled=True)  406 us
    psum x1, blocking collectives, per_device(): key_total, value_total = lax.psum((key_terms, value_terms), 'ctx')  302 us
    all_to_all x1, starting transfers between devices, per_device(): lax.all_to_all(jnp.stack(jnp.split(key_own.astype(jnp.bfloat16), lax.axis...  58.1 us
  transfers between devices with their start and end apart: 4, of which 3 were waited for; matrix products, arithmetic and copies ran while one was open for 2% of the time, Pallas kernels for 0%

profile of v1, /device:TPU:1, one launch (start us, length us, event | category | flops | bytes accessed | tf_op | source)
XLA Modules:
  0.0 1265.7 jit_solution(13012332923227250353)
XLA Ops:
  7.2 0.7 all-gather.7.cloned.1.call-update
  7.9 0.7 all-gather.5.cloned.1.call-update
  9.3 2.0 copy.200
  11.4 1.1 multiply_convert_fusion.1
  12.5 1.0 copy.201
  13.5 1.3 fusion.37
  14.9 1.3 compare_select_fusion.1
  16.3 410.5 %all-gather.7.cloned.1.call-done = bf16[256,2,4096]{2,1,0:T(2,128)(2,1)} async-done(((bf16[1,2,4096]{2,1,0:T(2,128)(2,1)}), bf16[256,2,4096]{2,1,0:T(2,128)(2,1)}) %all-gather.7.cloned.1.call-update) | async-done | bytes 4194320 | tf_op jit(solution)/shard_map/all_gather | solution.py:16
  426.8 7.2 reshape.211
  434.0 406.2 %all-gather.5.cloned.1.call-done = bf16[256,2,4096]{2,1,0:T(2,128)(2,1)} async-done(((bf16[1,2,4096]{2,1,0:T(2,128)(2,1)}), bf16[256,2,4096]{2,1,0:T(2,128)(2,1)}) %all-gather.5.cloned.1.call-update) | async-done | bytes 4194320 | tf_op jit(solution)/shard_map/all_gather | solution.py:17
  840.2 7.2 reshape.209
  847.5 1.7 constant_dynamic-slice_fusion
  850.3 4.2 fusion.39
  854.5 3.8 fusion.38
  858.3 3.6 fusion.17
  861.9 2.2 fusion.21
  864.1 8.6 fusion.7
  872.7 1.9 copy.186
  874.6 3.0 copy.189
  877.7 302.5 %all-reduce.2 = (bf16[512,1024]{1,0:T(8,128)(2,1)}, bf16[512,1024]{1,0:T(8,128)(2,1)}) all-reduce(f32[512,1024]{1,0:T(8,128)S(1)} %copy.186, f32[512,1024]{1,0:T(8,128)} %copy.189), channel_id=1, replica_groups=mesh['ctx'=64,'tp'=4] {'ctx'}, use_global_device_ids=true, to_apply=%region_3.4 | all-reduce | flops 1048576 | bytes 6291456 | tf_op jit(solution)/shard_map/psum | solution.py:78
  1180.1 0.7 dynamic-slice_convert_fusion.1
  1180.9 0.6 pad_maximum_fusion
  1181.5 58.1 %all-to-all-start = ((bf16[4,2,1024]{2,1,0:T(2,128)(2,1)}), bf16[4,2,1024]{2,1,0:T(2,128)(2,1)S(1)}, u32[]{:S(2)}, u32[]{:S(2)}) async-start(bf16[4,2,1024]{2,1,0:T(2,128)(2,1)} %pad_maximum_fusion), calls=%async_computation | async-start | bytes 32768 | tf_op jit(solution)/shard_map/all_to_all | solution.py:85
  1239.6 0.7 dynamic-slice_convert_fusion
  1240.3 0.6 all_to_all.14
  1240.9 3.3 all-to-all-done
  1244.2 3.9 all-to-all-start.1
  1248.2 7.4 fusion.18
  1255.6 1.0 copy.190
  1256.6 1.0 copy.191
  1257.6 0.6 convert_element_type.82
  1258.2 0.6 convert_element_type.83
  (23 shorter events, 1.4 us)
Async XLA Ops:
  7.2 419.6 %all-gather.7.cloned.1.call-start = ((), (), s32[]{:S(2)}) async-start(), calls=%async_computation.3 | async-start | bytes 4210688 | tf_op jit(solution)/shard_map/all_gather | solution.py:16
  7.9 832.3 %all-gather.5.cloned.1.call-start = ((), (), s32[]{:S(2)}) async-start(), calls=%async_computation.2 | async-start | bytes 4210688 | tf_op jit(solution)/shard_map/all_gather | solution.py:17
  850.3 8.0 copy-start.1
  850.3 4.2 copy-start.3
  858.3 3.6 copy-start
  858.3 3.6 copy-start.5
  874.6 373.6 %copy-start.2 = (bf16[512,1024]{0,1:T(8,128)(2,1)S(1)}, bf16[512,1024]{0,1:T(8,128)(2,1)}, u32[]{:S(2)}) copy-start(bf16[512,1024]{0,1:T(8,128)(2,1)} %copy-done.1) | copy-start | bytes 3145732
  1181.5 62.8 %all-to-all-start = ((bf16[4,2,1024]{2,1,0:T(2,128)(2,1)}), bf16[4,2,1024]{2,1,0:T(2,128)(2,1)S(1)}, u32[]{:S(2)}, u32[]{:S(2)}) async-start(bf16[4,2,1024]{2,1,0:T(2,128)(2,1)} %pad_maximum_fusion), calls=%async_computation | async-start | bytes 32768 | tf_op jit(solution)/shard_map/all_to_all | solution.py:85
  1244.2 14.0 %all-to-all-start.1 = ((bf16[4,2,1024]{2,1,0:T(2,128)(2,1)}), bf16[4,2,1024]{2,1,0:T(2,128)(2,1)S(1)}, u32[]{:S(2)}, u32[]{:S(2)}) async-start(bf16[4,2,1024]{2,1,0:T(2,128)(2,1)} %all_to_all.14), calls=%async_computation.1 | async-start | bytes 32768 | tf_op jit(solution)/shard_map/all_to_all | solution.py:93
  1248.2 7.4 copy-start.4
Sparse Core Ops, SparseCore 0:
  9.9 416.8 all-gather.6
  428.7 411.5 all-gather.4
